TPU v7x, 512 devices: a whole 4x4x16 slice. The times are simulated.
512 devices in a mesh: pipe: 4 (over y), seq: 16 (over z), tensor: 8 (over x, core).
Axes of the slice: x: 4, y: 4, z: 16, core: 2. Of those that a mesh axis runs over, the one named last changes fastest.
Arguments:
- layer_input: bfloat16 [4, 2048, 8192], P('pipe', 'seq', 'tensor'), may hold values from -320 to 320
- conv_out: bfloat16 [4, 2048, 8192], P('pipe', 'seq', 'tensor'), may hold values from -8 to 8
- act_grad: bfloat16 [4, 2048, 8192], P('pipe', 'seq', 'tensor'), may hold values from -6 to 6
- conv_kernel: bfloat16 [4, 4, 8192], P('pipe', None, 'tensor'), may hold values from -3 to 3
- in_proj: bfloat16 [4, 8192, 8192], P('pipe', 'seq', 'tensor'), may hold values from -0.0625 to 0.0625
- sketch_matrix: bfloat16 [4, 8192, 512], P('pipe', 'tensor'), may hold values from -0.0625 to 0.0625
Outputs:
- passed_grad: bfloat16 [4, 2048, 8192], P('pipe', 'tensor', 'seq')
- basis: bfloat16 [4, 8192, 512], P('pipe', 'tensor')
All inputs are finite; a program needn't handle non-finite values.
Results may differ from a plain program's by a relative error of at most 0.017.
Values may be sent and summed in bfloat16 or wider, within the bound.
No kernel may reach another device: no remote copies, remote signals or barrier semaphores. Data moves between devices by JAX's collectives and lax.ppermute only.
A program may use at most 64 MiB of HBM per device.

v0:
```python
import math
import jax
import jax.numpy as jnp
from jax import lax
from jax.sharding import PartitionSpec as P

D = 8192


def passed_along(block, axis, distance):
    devices = range(lax.axis_size(axis))
    route = [(i - distance, i) for i in devices if i - distance in devices]
    return lax.ppermute(block, axis, route)


def shifted(value, axis, by):
    count = lax.axis_size(axis)
    return lax.ppermute(value, axis, [(i, (i + by) % count) for i in range(count)])


def finish_basis(sketch, gram):
    low = jnp.linalg.cholesky(gram)
    ortho_t = lax.linalg.triangular_solve(low, sketch.T, left_side=True, lower=True)
    return (ortho_t.T * math.sqrt(D)).astype(jnp.bfloat16)


def local(layer_input, conv_out, act_grad, conv_kernel, in_proj, sketch_matrix):
    acts = layer_input[0]
    kernel = conv_kernel[0]
    weights = in_proj[0]
    test_matrix = sketch_matrix[0]
    tok_rows = acts.shape[0]
    taps = kernel.shape[0]
    pval = conv_out[0].astype(jnp.float32)
    sig = jax.nn.sigmoid(pval)
    pre_grad = act_grad[0].astype(jnp.float32) * sig * (1.0 + pval * (1.0 - sig))
    ahead = passed_along(pre_grad[: taps - 1], "seq", -1)
    extended = jnp.concatenate([pre_grad, ahead], axis=0)
    total = jnp.zeros(pre_grad.shape, jnp.float32)
    for tap in range(taps):
        total = total + kernel[tap].astype(jnp.float32) * extended[tap : tap + tok_rows]
    in_grad = total.astype(jnp.bfloat16)
    partial_grad = lax.dot_general(
        lax.all_gather(in_grad, "seq", axis=0, tiled=True),
        weights,
        (((1,), (1,)), ((), ())),
        preferred_element_type=jnp.float32,
    )
    input_grad = lax.psum_scatter(
        partial_grad.astype(jnp.bfloat16), "tensor", scatter_dimension=0, tiled=True
    )
    passed = shifted(input_grad, "pipe", -1)
    row_terms = jnp.dot(in_grad, test_matrix, preferred_element_type=jnp.float32)
    sketch_rows = lax.psum(row_terms, "tensor").astype(jnp.bfloat16)
    sketch_part = lax.dot_general(
        acts, sketch_rows, (((0,), (0,)), ((), ())), preferred_element_type=jnp.float32
    )
    sketch = lax.psum(sketch_part, "seq")
    gram_part = jnp.dot(sketch.T, sketch, precision=lax.Precision.HIGHEST)
    gram = lax.psum(gram_part, "tensor")
    basis = finish_basis(sketch, gram)
    return (passed[None], basis[None])


def solution(mesh):
    placed = (
        P("pipe", "seq", "tensor"),
        P("pipe", "seq", "tensor"),
        P("pipe", "seq", "tensor"),
        P("pipe", None, "tensor"),
        P("pipe", "seq", "tensor"),
        P("pipe", "tensor", None),
    )
    return jax.shard_map(
        local,
        mesh=mesh,
        in_specs=placed,
        out_specs=(P("pipe", "tensor", "seq"), P("pipe", "tensor", None)),
        check_vma=False,
    )
```

profile of v0, /device:TPU:26, one launch (start us, length us, event | category | flops | bytes accessed | tf_op | source)
XLA Modules:
  0.0 470.1 jit_solution(17740369245081746752)
XLA Ops:
  7.2 1.4 fusion.30
  8.7 1.3 collective-permute-start
  10.0 0.9 slice_convert_fusion.3
  10.8 3.5 collective-permute-done
  14.9 24.3 %all-reduce.8 = bf16[128,512]{1,0:T(8,128)(2,1)S(1)} all-reduce(f32[128,512]{1,0:T(8,128)S(1)} %fusion.15), channel_id=1, replica_groups=mesh['pipe'=4,'seq'=16,'tensor'=8] {'tensor'}, use_global_device_ids=true, to_apply=%region_1.0 | all-reduce | flops 65536 | bytes 393216 | tf_op jit(solution)/shard_map/psum | solution.py:54
  39.2 1.8 convolution_bitcast_fusion
  41.0 149.0 %all-reduce.5.cloned.1.call-done = f32[1024,512]{0,1:T(8,128)} async-done(((f32[1024,512]{0,1:T(8,128)}), f32[1024,512]{0,1:T(8,128)}) %all-reduce.5.cloned.1.call-update) | async-done | bytes 2097168 | tf_op jit(solution)/shard_map/psum | solution.py:58
  190.0 6.7 %fusion.56 = f32[512,512]{0,1:T(8,128)} fusion(f32[1024,512]{0,1:T(8,128)} %all-reduce.5.cloned.1.call-done), kind=kOutput, calls=%fused_computation.103 | convolution fusion | flops 3221225472 | bytes 3145728 | tf_op jit(solution)/shard_map/dot_general | solution.py:59
  196.8 0.7 all-gather.2.cloned.1.call-update
  198.0 70.5 %all-reduce.7.cloned.1.call-done = f32[512,512]{0,1:T(8,128)} async-done(((f32[512,512]{0,1:T(8,128)}), f32[512,512]{0,1:T(8,128)}) %all-reduce.7.cloned.1.call-update) | async-done | bytes 1048592 | tf_op jit(solution)/shard_map/psum | solution.py:60
  268.5 1.6 copy.9
  270.4 1.0 copy-done.7
  271.4 11.7 %cholesky.104 = f32[128,128]{1,0:T(8,128)S(1)} custom-call(f32[128,128]{1,0:T(8,128)S(1)} %cholesky.266), custom_call_target="Cholesky" | custom-call | tf_op jit(solution)/shard_map/jit(cholesky)/cholesky | solution.py:22
  283.3 9.8 %custom-call.30 = f32[1,128,128]{1,2,0:T(8,128)S(1)} custom-call(f32[1,128,128]{2,1,0:T(8,128)S(1)} %get-tuple-element.31), custom_call_target="InvertDiagBlocksLowerTriangular" | custom-call | tf_op jit(solution)/shard_map/jit(cholesky)/cholesky | solution.py:22
  293.1 1.2 constant_dynamic-update-slice_fusion.3
  294.4 1.3 convolution_subtract_fusion.2
  295.6 11.7 %cholesky.217 = f32[128,128]{1,0:T(8,128)S(1)} custom-call(f32[128,128]{1,0:T(8,128)S(1)} %cholesky.270), custom_call_target="Cholesky" | custom-call | tf_op jit(solution)/shard_map/jit(cholesky)/cholesky | solution.py:22
  307.4 10.0 %custom-call.31 = f32[1,128,128]{1,2,0:T(8,128)S(1)} custom-call(f32[1,128,128]{2,1,0:T(8,128)S(1)} %get-tuple-element.28), custom_call_target="InvertDiagBlocksLowerTriangular" | custom-call | tf_op jit(solution)/shard_map/jit(cholesky)/cholesky | solution.py:22
  317.6 1.4 convolution_subtract_fusion.3
  319.1 11.7 %cholesky.238 = f32[128,128]{1,0:T(8,128)S(1)} custom-call(f32[128,128]{1,0:T(8,128)S(1)} %cholesky.275), custom_call_target="Cholesky" | custom-call | tf_op jit(solution)/shard_map/jit(cholesky)/cholesky | solution.py:22
  330.8 21.4 %all-gather.2.cloned.1.call-done = bf16[2048,1024]{1,0:T(8,128)(2,1)} async-done(((bf16[128,1024]{1,0:T(8,128)(2,1)}), bf16[2048,1024]{1,0:T(8,128)(2,1)}) %all-gather.2.cloned.1.call-update) | async-done | bytes 4194320 | tf_op jit(solution)/shard_map/all_gather | solution.py:44
  352.2 5.9 %convolution_convert_fusion = bf16[2048,512]{1,0:T(8,128)(2,1)} fusion(bf16[2048,1024]{1,0:T(8,128)(2,1)} %all-gather.2.cloned.1.call-done, bf16[1,512,1024]{2,1,0:T(8,128)(2,1)S(1)} %copy-done), kind=kOutput, calls=%fused_computation.2 | convolution fusion | flops 2148532224 | bytes 7340032 | tf_op jit(solution)/shard_map/dot_general | solution.py:43
  358.1 0.6 select_reduce_fusion.1
  358.8 9.8 %custom-call.32 = f32[1,128,128]{1,2,0:T(8,128)S(1)} custom-call(f32[1,128,128]{2,1,0:T(8,128)S(1)} %get-tuple-element.25), custom_call_target="InvertDiagBlocksLowerTriangular" | custom-call | tf_op jit(solution)/shard_map/jit(cholesky)/cholesky | solution.py:22
  368.6 0.8 convolution_dynamic-update-slice_fusion.1
  369.4 1.5 convolution_subtract_fusion.4
  370.9 11.9 %cholesky.255 = f32[128,128]{1,0:T(8,128)S(1)} custom-call(f32[128,128]{1,0:T(8,128)S(1)} %convolution_subtract_fusion.4), custom_call_target="Cholesky" | custom-call | tf_op jit(solution)/shard_map/jit(cholesky)/cholesky | solution.py:22
  382.8 0.6 compare_reduce_fusion.2
  384.8 0.6 compare_reduce_fusion.1
  386.1 0.6 select_reduce_fusion
  386.7 0.6 compare_reduce_fusion
  388.0 2.3 select_select_fusion
  390.3 13.6 %while.1 = (s32[]{:T(128)}, f32[512,512]{1,0:T(8,128)}, s32[4,2]{0,1:T(2,128)S(1)}, f32[4,128,128]{2,1,0:T(8,128)}, s32[]{:T(128)}) while((s32[]{:T(128)}, f32[512,512]{1,0:T(8,128)}, s32[4,2]{0,1:T(2,128)S(1)}, f32[4,128,128]{2,1,0:T(8,128)}, s32[]{:T(128)}) %tuple.35), condition=%wide.while_cond, body=%wide.while_body.sunk | while | flops 2 | bytes 132205 | solution.py:23
  390.9 2.8 bitcast_dynamic-update-slice_fusion.2
  394.4 2.8 bitcast_dynamic-update-slice_fusion.2
  397.8 2.8 bitcast_dynamic-update-slice_fusion.2
  401.2 2.8 bitcast_dynamic-update-slice_fusion.2
  404.0 40.1 %custom-call.33 = f32[4,128,128]{1,2,0:T(8,128)S(1)} custom-call(f32[4,128,128]{2,1,0:T(8,128)} %get-tuple-element.9), custom_call_target="InvertDiagBlocksLowerTriangular" | custom-call | tf_op jit(solution)/shard_map/triangular_solve | solution.py:23
  444.8 1.5 convolution_subtract_fusion.1
  446.9 1.8 convolution_subtract_fusion
  449.4 0.8 copy-done.5
  450.1 2.8 fusion.7
  453.0 2.4 collective-permute-start.1
  455.4 1.7 fusion.44
  457.1 1.6 fusion.10
  458.8 1.3 copy.10
  460.1 2.6 collective-permute-done.1
  462.7 0.7 copy.32
  (53 shorter events, 6.3 us)
Async XLA Ops:
  7.2 345.0 %copy-start = (bf16[1,512,1024]{2,1,0:T(8,128)(2,1)S(1)}, bf16[1,512,1024]{2,1,0:T(8,128)(2,1)}, u32[]{:S(2)}) copy-start(bf16[1,512,1024]{2,1,0:T(8,128)(2,1)} %param.10) | copy-start | bytes 3145732
  7.2 7.4 %copy-start.9 = (bf16[1,1024,512]{2,1,0:T(8,128)(2,1)S(1)}, bf16[1,1024,512]{2,1,0:T(8,128)(2,1)}, u32[]{:S(2)}) copy-start(bf16[1,1024,512]{2,1,0:T(8,128)(2,1)} %param.11) | copy-start | bytes 3145732
  7.2 32.0 %copy-start.10 = (bf16[1,128,1024]{2,1,0:T(8,128)(2,1)S(1)}, bf16[1,128,1024]{2,1,0:T(8,128)(2,1)}, u32[]{:S(2)}) copy-start(bf16[1,128,1024]{2,1,0:T(8,128)(2,1)} %param.6) | copy-start | bytes 786436
  7.2 182.8 %all-reduce.5.cloned.1.call-start = ((), (), s32[]{:S(2)}) async-start(), calls=%async_computation.3 | async-start | bytes 4194304 | tf_op jit(solution)/shard_map/psum | solution.py:58
  8.7 5.6 %collective-permute-start = (f32[3,1024]{1,0:T(4,128)S(1)}, f32[3,1024]{1,0:T(4,128)S(1)}, u32[]{:S(2)}, u32[]{:S(2)}) collective-permute-start(f32[3,1024]{1,0:T(4,128)S(1)} %slice.150), channel_id=1, source_target_pairs={{8,0},{16,8},{24,16},{32,24},{40,32},{48,40},{56,48},{64,56},{72,6... | collective-permute-start | bytes 36872 | tf_op jit(solution)/shard_map/ppermute | solution.py:13
  14.5 26.4 %copy-start.8 = (bf16[128,1024]{1,0:T(8,128)(2,1)}, bf16[128,1024]{1,0:T(8,128)(2,1)S(1)}, u32[]{:S(2)}) copy-start(bf16[128,1024]{1,0:T(8,128)(2,1)S(1)} %fusion.22) | copy-start | bytes 786436
  41.0 227.5 %all-reduce.7.cloned.1.call-start = ((), (), s32[]{:S(2)}) async-start(), calls=%async_computation.4 | async-start | bytes 2097152 | tf_op jit(solution)/shard_map/psum | solution.py:60
  196.8 155.4 %all-gather.2.cloned.1.call-start = ((), (), s32[]{:S(2)}) async-start(), calls=%async_computation.1 | async-start | bytes 4456448 | tf_op jit(solution)/shard_map/all_gather | solution.py:44
  197.5 255.5 %reduce-scatter.2.cloned.1.call-start = ((), (), s32[]{:S(2)}) async-start(), calls=%async_computation.2 | async-start | bytes 2359296 | tf_op jit(solution)/shard_map/reduce_scatter | solution.py:49
  268.5 1.7 copy-start.6
  270.4 1.0 copy-start.7
  317.6 40.5 %copy-start.4 = (f32[512,512]{1,0:T(8,128)}, f32[512,512]{1,0:T(8,128)S(1)}, u32[]{:S(2)}) copy-start(f32[512,512]{1,0:T(8,128)S(1)} %convolution_dynamic-update-slice_fusion) | copy-start | bytes 3145732
  358.1 86.0 %copy-start.1 = (f32[1024,512]{0,1:T(8,128)S(1)}, f32[1024,512]{0,1:T(8,128)}, u32[]{:S(2)}) copy-start(f32[1024,512]{0,1:T(8,128)} %all-reduce.5.cloned.1.call-done) | copy-start | bytes 6291460
  444.8 4.6 copy-start.2
  446.9 2.4 copy-start.3
  449.3 0.8 copy-start.5
  453.0 9.7 %collective-permute-start.1 = (bf16[256,512]{1,0:T(8,128)(2,1)}, bf16[256,512]{1,0:T(8,128)(2,1)S(1)}, u32[]{:S(2)}, u32[]{:S(2)}) collective-permute-start(bf16[256,512]{1,0:T(8,128)(2,1)} %reduce-scatter.2.cloned.1.call-done), channel_id=1, source_target_pairs={{0,384},{128,0},{256,128},{384,256},{1,385},{129,1},{257,129},{385... | collective-permute-start | bytes 786440 | tf_op jit(solution)/shard_map/ppermute | solution.py:18
Sparse Core Ops, SparseCore 0:
  41.1 148.8 all-reduce.4
  196.9 71.6 all-reduce.6
  271.2 80.9 all-gather.1
  358.2 33.6 reduce-scatter.1
where the time goes:
time: 475 us; the launch traced here: 470 us
  waiting for transfers between devices  248 us (52%)
  other arithmetic  127 us (27%)
  matrix products  30.9 us (7%)
  blocking collectives  24.3 us (5%)
  local copies, waits for them, and re-layouts  19.3 us (4%)
  between operations  17 us (4%)
    psum x1, waiting for transfers between devices, local(): sketch = lax.psum(sketch_part, 'seq')  149 us
    another operation x14, other arithmetic, finish_basis(): low = jnp.linalg.cholesky(gram)  79.9 us
    psum x1, waiting for transfers between devices, local(): gram = lax.psum(gram_part, 'tensor')  70.5 us
    another operation x3, other arithmetic, finish_basis(): lax.linalg.triangular_solve(low, sketch.T, left_side=True, lower=True)  42.5 us
    psum x1, blocking collectives, local(): sketch_rows = lax.psum(row_terms, 'tensor').astype(jnp.bfloat16)  24.3 us
    all_gather x1, waiting for transfers between devices, local(): lax.all_gather(in_grad, 'seq', axis=0, tiled=True)  21.4 us
    another operation x12, local copies, waits for them, and re-layouts  13.6 us
    another operation x7, matrix products, finish_basis(): lax.linalg.triangular_solve(low, sketch.T, left_side=True, lower=True)  9.66 us
  transfers between devices with their start and end apart: 6, of which 5 were waited for; matrix products, arithmetic and copies ran while one was open for 34% of the time, Pallas kernels for 0%

commit v1 on v0

--- a/solution.py
+++ b/solution.py
@@ -5,6 +5,19 @@
 from jax.sharding import PartitionSpec as P
 
 D = 8192
+
+
+def gather_around(x, axis, dim):
+    ways = lax.axis_size(axis)
+    up = [(d, (d + 1) % ways) for d in range(ways)]
+    down = [(d, (d - 1) % ways) for d in range(ways)]
+    earlier, later = ([x], [x])
+    for _ in range(ways // 2):
+        earlier.append(lax.ppermute(earlier[-1], axis, up))
+    for _ in range((ways - 1) // 2):
+        later.append(lax.ppermute(later[-1], axis, down))
+    line = jnp.concatenate([*earlier[::-1], *later[1:]], axis=dim)
+    return jnp.roll(line, (lax.axis_index(axis) - ways // 2) * x.shape[dim], axis=dim)
 
 
 def passed_along(block, axis, distance):
@@ -41,7 +54,7 @@
         total = total + kernel[tap].astype(jnp.float32) * extended[tap : tap + tok_rows]
     in_grad = total.astype(jnp.bfloat16)
     partial_grad = lax.dot_general(
-        lax.all_gather(in_grad, "seq", axis=0, tiled=True),
+        gather_around(in_grad, "seq", 0),
         weights,
         (((1,), (1,)), ((), ())),
         preferred_element_type=jnp.float32,

time: 475 us -> 528 us (1.11)
  the two profiles are of different devices: /device:TPU:26 before, /device:TPU:31 now
where the time goes in v1:
time: 528 us; the launch traced here: 521 us
  waiting for transfers between devices  198 us (38%)
  other arithmetic  129 us (24%)
  local copies, waits for them, and re-layouts  55.8 us (11%)
  starting transfers between devices  54.3 us (10%)
  matrix products  35.1 us (7%)
  blocking collectives  32.4 us (6%)
  between operations  17 us (3%)
    psum x1, waiting for transfers between devices, local(): sketch = lax.psum(sketch_part, 'seq')  103 us
    another operation x14, other arithmetic, finish_basis(): low = jnp.linalg.cholesky(gram)  80.5 us
    psum x1, waiting for transfers between devices, local(): gram = lax.psum(gram_part, 'tensor')  67.1 us
    another operation x3, other arithmetic, finish_basis(): lax.linalg.triangular_solve(low, sketch.T, left_side=True, lower=True)  42.5 us
    unnamed x49, local copies, waits for them, and re-layouts  37.8 us
    ppermute x7, starting transfers between devices, gather_around(): later.append(lax.ppermute(later[-1], axis, down))  33 us
    psum x1, blocking collectives, local(): sketch_rows = lax.psum(row_terms, 'tensor').astype(jnp.bfloat16)  32.4 us
    ppermute x8, waiting for transfers between devices, gather_around(): earlier.append(lax.ppermute(earlier[-1], axis, up))  19.2 us
  transfers between devices with their start and end apart: 20, of which 10 were waited for; matrix products, arithmetic and copies ran while one was open for 40% of the time, Pallas kernels for 0%

profile of v1, /device:TPU:31, one launch (start us, length us, event | category | flops | bytes accessed | tf_op | source)
XLA Modules:
  0.0 521.1 jit_solution(7117792824593556437)
XLA Ops:
  10.7 2.5 collective-permute-done
  13.5 3.5 collective-permute-start.1
  17.0 11.5 %collective-permute-done.1 = bf16[128,1024]{1,0:T(8,128)(2,1)S(1)} collective-permute-done((bf16[128,1024]{1,0:T(8,128)(2,1)S(1)}, bf16[128,1024]{1,0:T(8,128)(2,1)S(1)}, u32[]{:S(2)}, u32[]{:S(2)}) %collective-permute-start.1) | collective-permute-done | bytes 262176 | tf_op jit(solution)/shard_map/ppermute | solution.py:16
  28.6 1.9 collective-permute-start.2
  30.5 4.6 collective-permute-start.9
  35.1 2.3 collective-permute-done.2
  37.3 1.9 collective-permute-start.3
  39.2 4.6 collective-permute-start.10
  43.8 1.8 collective-permute-done.3
  45.6 1.9 collective-permute-start.4
  47.6 4.6 collective-permute-start.11
  52.1 1.8 collective-permute-done.4
  53.9 1.9 collective-permute-start.5
  55.9 4.6 collective-permute-start.12
  62.3 1.9 collective-permute-start.6
  64.2 2.2 fusion.20
  66.4 4.6 collective-permute-start.13
  71.0 1.9 collective-permute-start.7
  72.9 32.4 %all-reduce.8 = bf16[128,512]{1,0:T(8,128)(2,1)S(1)} all-reduce(f32[128,512]{1,0:T(8,128)} %fusion.20), channel_id=1, replica_groups=mesh['pipe'=4,'seq'=16,'tensor'=8] {'tensor'}, use_global_device_ids=true, to_apply=%region_1.2 | all-reduce | flops 65536 | bytes 393216 | tf_op jit(solution)/shard_map/psum | solution.py:67
  105.4 4.9 collective-permute-start.14
  110.3 1.9 collective-permute-start.8
  112.2 2.8 convolution_bitcast_fusion
  116.4 5.3 %collective-permute-start.15 = (bf16[128,1024]{1,0:T(8,128)(2,1)}, bf16[128,1024]{1,0:T(8,128)(2,1)S(1)}, u32[]{:S(2)}, u32[]{:S(2)}) collective-permute-start(bf16[128,1024]{1,0:T(8,128)(2,1)} %collective-permute-done.14), channel_id=1, source_target_pairs={{0,120},{8,0},{16,8},{24,16},{32,24},{40,32},{48,40},{56,48},{64,5... | collective-permute-start | bytes 786440 | tf_op jit(solution)/shard_map/ppermute | solution.py:18
  148.5 103.1 %all-reduce.5.cloned.1.call-done = f32[1024,512]{0,1:T(8,128)} async-done(((f32[1024,512]{0,1:T(8,128)}), f32[1024,512]{0,1:T(8,128)}) %all-reduce.5.cloned.1.call-update) | async-done | bytes 2097168 | tf_op jit(solution)/shard_map/psum | solution.py:71
  251.6 6.7 %fusion.62 = f32[512,512]{0,1:T(8,128)} fusion(f32[1024,512]{0,1:T(8,128)} %all-reduce.5.cloned.1.call-done), kind=kOutput, calls=%fused_computation.138 | convolution fusion | flops 3221225472 | bytes 3145728 | tf_op jit(solution)/shard_map/dot_general | solution.py:72
  266.8 5.9 %fusion.2 = bf16[2048,512]{1,0:T(8,128)(2,1)} fusion(bf16[4096,1024]{1,0:T(8,128)(2,1)} %constant_dynamic-update-slice_fusion, s32[]{:T(128)S(6)} %select_n.18, bf16[1,512,1024]{2,1,0:T(8,128)(2,1)S(1)} %copy-done), kind=kOutput, calls=%fused_computation.4 | convolution fusion | flops 2148532224 | bytes 7340036 | tf_op jit(solution)/shard_map/dot_general | solution.py:56
  272.7 67.1 %all-reduce.7.cloned.1.call-done = f32[512,512]{0,1:T(8,128)} async-done(((f32[512,512]{0,1:T(8,128)}), f32[512,512]{0,1:T(8,128)}) %all-reduce.7.cloned.1.call-update) | async-done | bytes 1048592 | tf_op jit(solution)/shard_map/psum | solution.py:73
  339.8 2.5 copy.9
  342.3 1.8 fusion.19
  345.1 11.7 %cholesky.104 = f32[128,128]{1,0:T(8,128)S(1)} custom-call(f32[128,128]{1,0:T(8,128)S(1)} %cholesky.266), custom_call_target="Cholesky" | custom-call | tf_op jit(solution)/shard_map/jit(cholesky)/cholesky | solution.py:35
  357.9 9.8 %custom-call.30 = f32[1,128,128]{1,2,0:T(8,128)S(1)} custom-call(f32[1,128,128]{2,1,0:T(8,128)S(1)} %get-tuple-element.31), custom_call_target="InvertDiagBlocksLowerTriangular" | custom-call | tf_op jit(solution)/shard_map/jit(cholesky)/cholesky | solution.py:35
  367.7 1.9 constant_dynamic-update-slice_fusion.35
  370.9 11.9 %cholesky.217 = f32[128,128]{1,0:T(8,128)S(1)} custom-call(f32[128,128]{1,0:T(8,128)S(1)} %cholesky.270), custom_call_target="Cholesky" | custom-call | tf_op jit(solution)/shard_map/jit(cholesky)/cholesky | solution.py:35
  383.4 9.8 %custom-call.31 = f32[1,128,128]{1,2,0:T(8,128)S(1)} custom-call(f32[1,128,128]{2,1,0:T(8,128)S(1)} %get-tuple-element.28), custom_call_target="InvertDiagBlocksLowerTriangular" | custom-call | tf_op jit(solution)/shard_map/jit(cholesky)/cholesky | solution.py:35
  395.6 11.7 %cholesky.238 = f32[128,128]{1,0:T(8,128)S(1)} custom-call(f32[128,128]{1,0:T(8,128)S(1)} %cholesky.275), custom_call_target="Cholesky" | custom-call | tf_op jit(solution)/shard_map/jit(cholesky)/cholesky | solution.py:35
  408.0 9.8 %custom-call.32 = f32[1,128,128]{1,2,0:T(8,128)S(1)} custom-call(f32[1,128,128]{2,1,0:T(8,128)S(1)} %get-tuple-element.25), custom_call_target="InvertDiagBlocksLowerTriangular" | custom-call | tf_op jit(solution)/shard_map/jit(cholesky)/cholesky | solution.py:35
  420.0 11.9 %cholesky.255 = f32[128,128]{1,0:T(8,128)S(1)} custom-call(f32[128,128]{1,0:T(8,128)S(1)} %convolution_subtract_fusion.4), custom_call_target="Cholesky" | custom-call | tf_op jit(solution)/shard_map/jit(cholesky)/cholesky | solution.py:35
  437.0 2.3 select_select_fusion
  439.4 13.7 %while.1 = (s32[]{:T(128)}, f32[512,512]{1,0:T(8,128)}, s32[4,2]{0,1:T(2,128)S(1)}, f32[4,128,128]{2,1,0:T(8,128)}, s32[]{:T(128)}) while((s32[]{:T(128)}, f32[512,512]{1,0:T(8,128)}, s32[4,2]{0,1:T(2,128)S(1)}, f32[4,128,128]{2,1,0:T(8,128)}, s32[]{:T(128)}) %tuple.35), condition=%wide.while_cond, body=%wide.while_body.sunk | while | flops 2 | bytes 132205 | solution.py:36
  440.0 2.8 bitcast_dynamic-update-slice_fusion.2
  443.4 2.8 bitcast_dynamic-update-slice_fusion.2
  446.8 2.8 bitcast_dynamic-update-slice_fusion.2
  450.3 2.8 bitcast_dynamic-update-slice_fusion.2
  453.1 40.1 %custom-call.33 = f32[4,128,128]{1,2,0:T(8,128)S(1)} custom-call(f32[4,128,128]{2,1,0:T(8,128)} %get-tuple-element.9), custom_call_target="InvertDiagBlocksLowerTriangular" | custom-call | tf_op jit(solution)/shard_map/triangular_solve | solution.py:36
  496.0 1.8 convolution_subtract_fusion
  499.2 2.8 fusion.12
  502.0 2.4 collective-permute-start.16
  509.1 4.5 collective-permute-done.16
  (106 shorter events, 65.9 us)
Async XLA Ops:
  7.2 259.6 %copy-start = (bf16[1,512,1024]{2,1,0:T(8,128)(2,1)S(1)}, bf16[1,512,1024]{2,1,0:T(8,128)(2,1)}, u32[]{:S(2)}) copy-start(bf16[1,512,1024]{2,1,0:T(8,128)(2,1)} %param.10) | copy-start | bytes 3145732
  7.2 244.4 %all-reduce.5.cloned.1.call-start = ((), (), s32[]{:S(2)}) async-start(), calls=%async_computation.2 | async-start | bytes 4194304 | tf_op jit(solution)/shard_map/psum | solution.py:71
  8.6 4.7 collective-permute-start
  13.5 15.1 %collective-permute-start.1 = (bf16[128,1024]{1,0:T(8,128)(2,1)S(1)}, bf16[128,1024]{1,0:T(8,128)(2,1)S(1)}, u32[]{:S(2)}, u32[]{:S(2)}) collective-permute-start(bf16[128,1024]{1,0:T(8,128)(2,1)S(1)} %fusion.27), channel_id=1, source_target_pairs={{0,8},{8,16},{16,24},{24,32},{32,40},{40,48},{48,56},{56,64},{64,7... | collective-permute-start | bytes 786440 | tf_op jit(solution)/shard_map/ppermute | solution.py:16
  28.6 8.8 %collective-permute-start.2 = (bf16[128,1024]{1,0:T(8,128)(2,1)S(1)}, bf16[128,1024]{1,0:T(8,128)(2,1)S(1)}, u32[]{:S(2)}, u32[]{:S(2)}) collective-permute-start(bf16[128,1024]{1,0:T(8,128)(2,1)S(1)} %collective-permute-done.1), channel_id=1, source_target_pairs={{0,8},{8,16},{16,24},{24,32},{32,40},{40,48},{48,56},{56,64},{64,7... | collective-permute-start | bytes 786440 | tf_op jit(solution)/shard_map/ppermute | solution.py:16
  30.5 8.8 %collective-permute-start.9 = (bf16[128,1024]{1,0:T(8,128)(2,1)S(1)}, bf16[128,1024]{1,0:T(8,128)(2,1)S(1)}, u32[]{:S(2)}, u32[]{:S(2)}) collective-permute-start(bf16[128,1024]{1,0:T(8,128)(2,1)S(1)} %fusion.27), channel_id=1, source_target_pairs={{0,120},{8,0},{16,8},{24,16},{32,24},{40,32},{48,40},{56,48},{64,5... | collective-permute-start | bytes 786440 | tf_op jit(solution)/shard_map/ppermute | solution.py:18
  37.3 8.3 %collective-permute-start.3 = (bf16[128,1024]{1,0:T(8,128)(2,1)S(1)}, bf16[128,1024]{1,0:T(8,128)(2,1)S(1)}, u32[]{:S(2)}, u32[]{:S(2)}) collective-permute-start(bf16[128,1024]{1,0:T(8,128)(2,1)S(1)} %collective-permute-done.2), channel_id=1, source_target_pairs={{0,8},{8,16},{16,24},{24,32},{32,40},{40,48},{48,56},{56,64},{64,7... | collective-permute-start | bytes 786440 | tf_op jit(solution)/shard_map/ppermute | solution.py:16
  39.2 8.3 %collective-permute-start.10 = (bf16[128,1024]{1,0:T(8,128)(2,1)S(1)}, bf16[128,1024]{1,0:T(8,128)(2,1)S(1)}, u32[]{:S(2)}, u32[]{:S(2)}) collective-permute-start(bf16[128,1024]{1,0:T(8,128)(2,1)S(1)} %collective-permute-done.9), channel_id=1, source_target_pairs={{0,120},{8,0},{16,8},{24,16},{32,24},{40,32},{48,40},{56,48},{64,5... | collective-permute-start | bytes 786440 | tf_op jit(solution)/shard_map/ppermute | solution.py:18
  45.6 8.3 %collective-permute-start.4 = (bf16[128,1024]{1,0:T(8,128)(2,1)S(1)}, bf16[128,1024]{1,0:T(8,128)(2,1)S(1)}, u32[]{:S(2)}, u32[]{:S(2)}) collective-permute-start(bf16[128,1024]{1,0:T(8,128)(2,1)S(1)} %collective-permute-done.3), channel_id=1, source_target_pairs={{0,8},{8,16},{16,24},{24,32},{32,40},{40,48},{48,56},{56,64},{64,7... | collective-permute-start | bytes 786440 | tf_op jit(solution)/shard_map/ppermute | solution.py:16
  47.6 8.4 %collective-permute-start.11 = (bf16[128,1024]{1,0:T(8,128)(2,1)S(1)}, bf16[128,1024]{1,0:T(8,128)(2,1)S(1)}, u32[]{:S(2)}, u32[]{:S(2)}) collective-permute-start(bf16[128,1024]{1,0:T(8,128)(2,1)S(1)} %collective-permute-done.10), channel_id=1, source_target_pairs={{0,120},{8,0},{16,8},{24,16},{32,24},{40,32},{48,40},{56,48},{64,5... | collective-permute-start | bytes 786440 | tf_op jit(solution)/shard_map/ppermute | solution.py:18
  53.9 8.3 %collective-permute-start.5 = (bf16[128,1024]{1,0:T(8,128)(2,1)S(1)}, bf16[128,1024]{1,0:T(8,128)(2,1)S(1)}, u32[]{:S(2)}, u32[]{:S(2)}) collective-permute-start(bf16[128,1024]{1,0:T(8,128)(2,1)S(1)} %collective-permute-done.4), channel_id=1, source_target_pairs={{0,8},{8,16},{16,24},{24,32},{32,40},{40,48},{48,56},{56,64},{64,7... | collective-permute-start | bytes 786440 | tf_op jit(solution)/shard_map/ppermute | solution.py:16
  55.9 10.5 %collective-permute-start.12 = (bf16[128,1024]{1,0:T(8,128)(2,1)S(1)}, bf16[128,1024]{1,0:T(8,128)(2,1)}, u32[]{:S(2)}, u32[]{:S(2)}) collective-permute-start(bf16[128,1024]{1,0:T(8,128)(2,1)S(1)} %collective-permute-done.11), channel_id=1, source_target_pairs={{0,120},{8,0},{16,8},{24,16},{32,24},{40,32},{48,40},{56,48},{64,5... | collective-permute-start | bytes 786440 | tf_op jit(solution)/shard_map/ppermute | solution.py:18
  62.3 8.7 %collective-permute-start.6 = (bf16[128,1024]{1,0:T(8,128)(2,1)S(1)}, bf16[128,1024]{1,0:T(8,128)(2,1)}, u32[]{:S(2)}, u32[]{:S(2)}) collective-permute-start(bf16[128,1024]{1,0:T(8,128)(2,1)S(1)} %collective-permute-done.5), channel_id=1, source_target_pairs={{0,8},{8,16},{16,24},{24,32},{32,40},{40,48},{48,56},{56,64},{64,7... | collective-permute-start | bytes 786440 | tf_op jit(solution)/shard_map/ppermute | solution.py:16
  66.4 39.0 %collective-permute-start.13 = (bf16[128,1024]{1,0:T(8,128)(2,1)}, bf16[128,1024]{1,0:T(8,128)(2,1)}, u32[]{:S(2)}, u32[]{:S(2)}) collective-permute-start(bf16[128,1024]{1,0:T(8,128)(2,1)} %collective-permute-done.12), channel_id=1, source_target_pairs={{0,120},{8,0},{16,8},{24,16},{32,24},{40,32},{48,40},{56,48},{64,5... | collective-permute-start | bytes 786440 | tf_op jit(solution)/shard_map/ppermute | solution.py:18
  71.0 39.2 %collective-permute-start.7 = (bf16[128,1024]{1,0:T(8,128)(2,1)}, bf16[128,1024]{1,0:T(8,128)(2,1)}, u32[]{:S(2)}, u32[]{:S(2)}) collective-permute-start(bf16[128,1024]{1,0:T(8,128)(2,1)} %collective-permute-done.6), channel_id=1, source_target_pairs={{0,8},{8,16},{16,24},{24,32},{32,40},{40,48},{48,56},{56,64},{64,7... | collective-permute-start | bytes 786440 | tf_op jit(solution)/shard_map/ppermute | solution.py:16
  105.4 11.1 %collective-permute-start.14 = (bf16[128,1024]{1,0:T(8,128)(2,1)}, bf16[128,1024]{1,0:T(8,128)(2,1)}, u32[]{:S(2)}, u32[]{:S(2)}) collective-permute-start(bf16[128,1024]{1,0:T(8,128)(2,1)} %collective-permute-done.13), channel_id=1, source_target_pairs={{0,120},{8,0},{16,8},{24,16},{32,24},{40,32},{48,40},{56,48},{64,5... | collective-permute-start | bytes 786440 | tf_op jit(solution)/shard_map/ppermute | solution.py:18
  110.3 11.5 %collective-permute-start.8 = (bf16[128,1024]{1,0:T(8,128)(2,1)}, bf16[128,1024]{1,0:T(8,128)(2,1)}, u32[]{:S(2)}, u32[]{:S(2)}) collective-permute-start(bf16[128,1024]{1,0:T(8,128)(2,1)} %collective-permute-done.7), channel_id=1, source_target_pairs={{0,8},{8,16},{16,24},{24,32},{32,40},{40,48},{48,56},{56,64},{64,7... | collective-permute-start | bytes 786440 | tf_op jit(solution)/shard_map/ppermute | solution.py:16
  115.0 224.7 %all-reduce.7.cloned.1.call-start = ((), (), s32[]{:S(2)}) async-start(), calls=%async_computation.3 | async-start | bytes 2097152 | tf_op jit(solution)/shard_map/psum | solution.py:73
  116.4 21.9 %collective-permute-start.15 = (bf16[128,1024]{1,0:T(8,128)(2,1)}, bf16[128,1024]{1,0:T(8,128)(2,1)S(1)}, u32[]{:S(2)}, u32[]{:S(2)}) collective-permute-start(bf16[128,1024]{1,0:T(8,128)(2,1)} %collective-permute-done.14), channel_id=1, source_target_pairs={{0,120},{8,0},{16,8},{24,16},{32,24},{40,32},{48,40},{56,48},{64,5... | collective-permute-start | bytes 786440 | tf_op jit(solution)/shard_map/ppermute | solution.py:18
  138.3 9.5 %copy-start.6 = (bf16[128,1024]{1,0:T(8,128)(2,1)}, bf16[128,1024]{1,0:T(8,128)(2,1)S(1)}, u32[]{:S(2)}) copy-start(bf16[128,1024]{1,0:T(8,128)(2,1)S(1)} %collective-permute-done.15) | copy-start | bytes 786436
  148.5 117.5 %copy-start.7 = (bf16[128,1024]{1,0:T(8,128)(2,1)S(1)}, bf16[128,1024]{1,0:T(8,128)(2,1)}, u32[]{:S(2)}) copy-start(bf16[128,1024]{1,0:T(8,128)(2,1)} %copy-done.6) | copy-start | bytes 786436
  258.3 243.8 %reduce-scatter.2.cloned.1.call-start = ((), (), s32[]{:S(2)}) async-start(), calls=%async_computation.1 | async-start | bytes 2359296 | tf_op jit(solution)/shard_map/reduce_scatter | solution.py:62
  272.7 220.5 %copy-start.1 = (f32[1024,512]{0,1:T(8,128)S(1)}, f32[1024,512]{0,1:T(8,128)}, u32[]{:S(2)}) copy-start(f32[1024,512]{0,1:T(8,128)} %all-reduce.5.cloned.1.call-done) | copy-start | bytes 6291460
  344.1 1.0 copy-start.5
  493.8 4.6 copy-start.2
  496.0 2.4 copy-start.3
  498.4 0.8 copy-start.4
  502.0 11.6 %collective-permute-start.16 = (bf16[256,512]{1,0:T(8,128)(2,1)}, bf16[256,512]{1,0:T(8,128)(2,1)S(1)}, u32[]{:S(2)}, u32[]{:S(2)}) collective-permute-start(bf16[256,512]{1,0:T(8,128)(2,1)} %reduce-scatter.2.cloned.1.call-done), channel_id=1, source_target_pairs={{0,384},{128,0},{256,128},{384,256},{1,385},{129,1},{257,129},{385... | collective-permute-start | bytes 786440 | tf_op jit(solution)/shard_map/ppermute | solution.py:31
Sparse Core Ops, SparseCore 0:
  115.2 136.3 all-reduce.4
  258.4 81.3 all-reduce.6
  342.6 40.2 reduce-scatter.1
